TPU v7x, 32 devices: a whole 2x2x4 slice. The times are simulated.
32 devices in a mesh: feed: 4 (over y, core), chan: 8 (over z, x).
Axes of the slice: x: 2, y: 2, z: 4, core: 2. Of those that a mesh axis runs over, the one named last changes fastest.
Arguments:
- voltages: bfloat16 [2, 2, 8, 4096, 1024], P(None, None, 'chan', None, 'feed'), may hold values from -6 to 6
- history: bfloat16 [2, 2, 8, 48, 1024], P(None, None, 'chan', None, 'feed'), may hold values from -6 to 6
- gains: float32 [2, 2, 8, 1024], P(None, None, 'chan', 'feed'), may hold values from -4 to 4
- weights: bfloat16 [2, 8, 1024, 1024], P(None, 'chan'), may hold values from -0.09375 to 0.09375
- beam_lists: int32 [8, 256], replicated, may hold values from 0 to 1023, as said below
- beam_counts: int32 [8], replicated, may hold values from 1 to 256, as said below
Outputs:
- power_blocks: bfloat16 [128, 128, 2048], P('feed', None, 'chan')
Inputs may be any that keep to these rules, and one draw needn't show every extreme that they name: `beam_lists`: row n holds in its first beam_counts[n] entries, in increasing order, the beams that node n owns, and 0 in the others; every beam is owned by exactly one node. `beam_counts`: the counts sum to 1024; some node owns exactly 256 beams.
All inputs are finite; a program needn't handle non-finite values.
Results may differ from a plain program's by a relative error of at most 0.013.
Values may be sent and summed in bfloat16 or wider, within the bound.
A program may use at most 192 MiB of HBM per device.

v0:
```python
import functools
import math

import jax
import jax.numpy as jnp
import ml_dtypes
import numpy as np
from jax import lax
from jax.experimental import pallas as pl
from jax.experimental.pallas import tpu as pltpu
from jax.sharding import PartitionSpec as P

U = 16
TAPS = 4
TINT = 2
GROUP = 4
WINDOW = 2 * GROUP
PAST = (TAPS - 1) * U
CHUNKS = 8


def filterbank_table():
    length = TAPS * U
    positions = np.arange(length, dtype=np.float64)
    offsets = (positions - (length - 1) / 2.0) / U
    taper = 0.5 - 0.5 * np.cos(2.0 * math.pi * (positions + 0.5) / length)
    window = np.sinc(offsets) * taper
    window = (window / np.sqrt(np.sum(window * window) / U)).reshape(TAPS, U)
    index_n = np.arange(U)
    phases = 2.0 * math.pi * (index_n[:, None] * index_n[None, :] % U) / U
    cosine, sine = np.cos(phases) / math.sqrt(U), np.sin(phases) / math.sqrt(U)
    parts = [[cosine, -sine], [sine, cosine]]
    table = np.zeros((2, GROUP, U, 2, WINDOW, U))
    for part_in in range(2):
        for part_out in range(2):
            for spectrum in range(GROUP):
                for tap in range(TAPS):
                    table[part_out, spectrum, :, part_in, spectrum + tap, :] = (
                        window[tap][:, None] * parts[part_in][part_out]
                    ).T
    return table.reshape(2 * GROUP * U, 2 * WINDOW * U).astype(ml_dtypes.bfloat16)


def kernel(
    feed_n,
    chan_n,
    table_ref,
    gains_ref,
    lists_ref,
    counts_ref,
    volt_ref,
    hist_ref,
    weight_ref,
    out_ref,
    xbuf,
    stage,
    recv,
    wbuf,
    pick,
    det,
    pstage,
    main_sem,
    past_sem,
    w_sem,
    feed_send,
    feed_recv,
    chan_send,
    chan_recv,
    self_sem,
):
    me_f, me_c = lax.axis_index("feed"), lax.axis_index("chan")
    chips = feed_n // 2
    my_y, my_core = me_f // 2, me_f % 2
    hops = [(dy, dc) for dy in range(1, chips) for dc in range(2)] + [(0, 1), (0, 0)]
    far = len(hops) - 2
    dests = [lax.rem(my_y + dy, chips) * 2 + lax.rem(my_core + dc, 2) for dy, dc in hops]
    nodes = [lax.rem(me_c + step, chan_n) for step in range(1, chan_n)]

    block = volt_ref.shape[3] // feed_n
    feeds = volt_ref.shape[4]
    beams = weight_ref.shape[3]
    slots = lists_ref.shape[1]
    span = block // CHUNKS
    rows = 2 * span
    bins = span // U // TINT

    barrier = pltpu.get_barrier_semaphore()
    for dest in dests[:-1]:
        pl.semaphore_signal(
            barrier, inc=1, device_id={"feed": dest}, device_id_type=pl.DeviceIdType.MESH
        )
    for node in nodes:
        pl.semaphore_signal(
            barrier, inc=1, device_id={"chan": node}, device_id_type=pl.DeviceIdType.MESH
        )

    def main_copy(o):
        return pltpu.make_async_copy(
            volt_ref.at[:, :, 0, pl.ds(pl.multiple_of(dests[o] * block, U), block), :],
            xbuf.at[o, :, :, pl.ds(PAST, block), :],
            main_sem.at[o],
        )

    def past_copy(o):
        return pltpu.make_async_copy(
            hist_ref.at[:, :, 0, :, :], xbuf.at[o, :, :, pl.ds(0, PAST), :], past_sem.at[o]
        )

    for o in range(feed_n):
        main_copy(o).start()

        @pl.when(dests[o] == 0)
        def _():
            past_copy(o).start()

        @pl.when(dests[o] > 0)
        def _():
            first = pl.multiple_of(jnp.maximum(dests[o], 1) * block - PAST, U)
            pltpu.make_async_copy(
                volt_ref.at[:, :, 0, pl.ds(first, PAST), :],
                xbuf.at[o, :, :, pl.ds(0, PAST), :],
                past_sem.at[o],
            ).start()

        xbuf[o, :, :, pl.ds(PAST + block, U), :] = jnp.zeros((2, 2, U, feeds), jnp.bfloat16)

    w_copy = pltpu.make_async_copy(weight_ref.at[:, 0], wbuf, w_sem)
    w_copy.start()

    pl.semaphore_wait(barrier, feed_n - 1 + chan_n - 1)

    def filterbank(o, q):
        for group in range(span // U // GROUP):
            first = pl.multiple_of(q * span + group * GROUP * U, U)
            for pol in range(2):
                window = jnp.concatenate(
                    [xbuf[o, part, pol, pl.ds(first, WINDOW * U), :] for part in range(2)], axis=0
                )
                spectrum = jnp.dot(table_ref[...], window, preferred_element_type=jnp.float32)
                half = GROUP * U
                re, im = spectrum[:half], spectrum[half:]
                gain_re, gain_im = gains_ref[0, pol, :, :], gains_ref[1, pol, :, :]
                cal = (gain_re * re - gain_im * im, gain_re * im + gain_im * re)
                at = pl.ds(pol * span + group * half, half)
                for part in range(2):
                    if o == feed_n - 1:
                        lanes = pl.ds(pl.multiple_of(me_f * feeds, 128), feeds)
                        recv[q, part, at, lanes] = cal[part].astype(jnp.bfloat16)
                    else:
                        stage[o, q, part, at, :] = cal[part].astype(jnp.bfloat16)

    def feed_copy(o, q):
        return pltpu.make_async_remote_copy(
            src_ref=stage.at[o, q],
            dst_ref=recv.at[q, :, :, pl.ds(pl.multiple_of(me_f * feeds, 128), feeds)],
            send_sem=feed_send.at[o, q],
            recv_sem=feed_recv.at[o, q],
            device_id={"feed": dests[o]},
            device_id_type=pl.DeviceIdType.MESH,
        )

    def chan_copy(step, q):
        node = nodes[step]
        return pltpu.make_async_remote_copy(
            src_ref=pstage.at[q, node],
            dst_ref=out_ref.at[pl.ds(q * bins, bins), pl.ds(pl.multiple_of(me_c * U, U), U), :],
            send_sem=chan_send.at[step, q],
            recv_sem=chan_recv.at[step, q],
            device_id={"chan": node},
            device_id_type=pl.DeviceIdType.MESH,
        )

    def self_copy(q):
        return pltpu.make_async_copy(
            pstage.at[q, me_c],
            out_ref.at[pl.ds(q * bins, bins), pl.ds(pl.multiple_of(me_c * U, U), U), :],
            self_sem.at[q],
        )

    for o in range(far):
        main_copy(o).wait()
        past_copy(o).wait()

    def far_step(q, carry):
        for o in range(far):
            filterbank(o, q)
            feed_copy(o, q).start()
        return carry

    lax.fori_loop(0, CHUNKS, far_step, 0)

    for o in range(far, feed_n):
        main_copy(o).wait()
        past_copy(o).wait()

    def near_step(q, carry):
        filterbank(far, q)
        feed_copy(far, q).start()
        filterbank(far + 1, q)
        return carry

    lax.fori_loop(0, CHUNKS, near_step, 0)

    for node in range(chan_n):
        slot = lax.broadcasted_iota(jnp.int32, (1, slots), 1)
        owned = jnp.where(slot < counts_ref[node], lists_ref[pl.ds(node, 1), :], -1)
        beam = lax.broadcasted_iota(jnp.int32, (beams, slots), 0)
        pick[node] = jnp.where(beam == owned, 1.0, 0.0).astype(jnp.bfloat16)

    w_copy.wait()
    tile = 256

    def beam_step(q, carry):
        for o in range(feed_n - 1):
            feed_copy(o, q).wait_recv()

        def columns(n, inner):
            at = pl.ds(pl.multiple_of(n * tile, tile), tile)
            w_re, w_im = wbuf[0, :, at], wbuf[1, :, at]
            c_re, c_im = recv[q, 0], recv[q, 1]
            dot = functools.partial(jnp.dot, preferred_element_type=jnp.float32)
            re = dot(c_re, w_re) - dot(c_im, w_im)
            im = dot(c_re, w_im) + dot(c_im, w_re)
            power = (re * re + im * im).reshape(2, bins, TINT, U, tile)
            power = jnp.sum(power[0] + power[1], axis=1) * (1.0 / (4.0 * TINT))
            det[:, at] = power.reshape(bins * U, tile).astype(jnp.bfloat16)
            return inner

        lax.fori_loop(0, beams // tile, columns, 0)
        for node in range(chan_n):
            picked = jnp.dot(det[...], pick[node], preferred_element_type=jnp.float32)
            pstage[q, node] = picked.astype(jnp.bfloat16).reshape(bins, U, slots)
        for step in range(chan_n - 1):
            chan_copy(step, q).start()
        self_copy(q).start()
        return carry

    lax.fori_loop(0, CHUNKS, beam_step, 0)

    def finish(q, carry):
        for o in range(feed_n - 1):
            feed_copy(o, q).wait_send()
        for step in range(chan_n - 1):
            chan_copy(step, q).wait()
        self_copy(q).wait()
        return carry

    lax.fori_loop(0, CHUNKS, finish, 0)


def on_device(feed_n, chan_n, voltages, history, gains, weights, beam_lists, beam_counts):
    samples, feeds = voltages.shape[3], voltages.shape[4]
    total_feeds, beams = weights.shape[2], weights.shape[3]
    slots = beam_lists.shape[1]
    block = samples // feed_n
    span = block // CHUNKS
    bins = span // U // TINT
    bf16 = jnp.bfloat16
    vmem = pl.BlockSpec(memory_space=pltpu.VMEM)
    hbm = pl.BlockSpec(memory_space=pl.ANY)
    spectra = samples // U
    flops = 2 * 4 * 2 * (block // U) * U * total_feeds * beams
    return pl.pallas_call(
        functools.partial(kernel, feed_n, chan_n),
        out_shape=jax.ShapeDtypeStruct((block // U // TINT, chan_n * U, slots), bf16),
        in_specs=[vmem, vmem, vmem, pl.BlockSpec(memory_space=pltpu.SMEM), hbm, hbm, hbm],
        out_specs=hbm,
        scratch_shapes=[
            pltpu.VMEM((feed_n, 2, 2, PAST + block + U, feeds), bf16),
            pltpu.VMEM((feed_n - 1, CHUNKS, 2, 2 * span, feeds), bf16),
            pltpu.VMEM((CHUNKS, 2, 2 * span, total_feeds), bf16),
            pltpu.VMEM((2, total_feeds, beams), bf16),
            pltpu.VMEM((chan_n, beams, slots), bf16),
            pltpu.VMEM((bins * U, beams), bf16),
            pltpu.VMEM((CHUNKS, chan_n, bins, U, slots), bf16),
            pltpu.SemaphoreType.DMA((feed_n,)),
            pltpu.SemaphoreType.DMA((feed_n,)),
            pltpu.SemaphoreType.DMA,
            pltpu.SemaphoreType.DMA((feed_n - 1, CHUNKS)),
            pltpu.SemaphoreType.DMA((feed_n - 1, CHUNKS)),
            pltpu.SemaphoreType.DMA((chan_n - 1, CHUNKS)),
            pltpu.SemaphoreType.DMA((chan_n - 1, CHUNKS)),
            pltpu.SemaphoreType.DMA((CHUNKS,)),
        ],
        compiler_params=pltpu.CompilerParams(
            collective_id=0, has_side_effects=True, vmem_limit_bytes=56 * 2**20
        ),
        cost_estimate=pl.CostEstimate(
            flops=flops, bytes_accessed=4 * spectra * U * feeds * 2 + 4 * total_feeds * beams, transcendentals=0
        ),
    )(
        jnp.asarray(filterbank_table()),
        gains.reshape(2, 2, 1, feeds),
        beam_lists,
        beam_counts,
        voltages,
        history,
        weights,
    )


def solution(mesh):
    in_specs = (
        P(None, None, "chan", None, "feed"),
        P(None, None, "chan", None, "feed"),
        P(None, None, "chan", "feed"),
        P(None, "chan", None, None),
        P(),
        P(),
    )
    out_specs = P("feed", None, "chan")
    body = functools.partial(on_device, mesh.shape["feed"], mesh.shape["chan"])
    return jax.shard_map(body, mesh=mesh, in_specs=in_specs, out_specs=out_specs, check_vma=False)
```

profile of v0, /device:TPU:0, one launch (start us, length us, event | category | flops | bytes accessed | tf_op | source)
XLA Modules:
  0.0 111.7 jit_solution(3248455611884045209)
XLA Ops:
  0.0 108.6 %shard_map.73 = bf16[32,128,256]{2,1,0:T(8,128)(2,1)} custom-call(bf16[128,256]{1,0:T(8,128)(2,1)} %constant.2.clone.table_ref, f32[2,2,1,256]{3,2,1,0:T(1,128)} %gains_ref.1, s32[8,256]{1,0:T(8,128)} %lists_ref.1, s32[8]{0:T(128)} %counts_ref.1, bf16[2,2,1,4096,256]{4,3,2,1,0:T(8,128)(2,1)} %volt_ref.1, bf16[2,2,1,48,256]{4,3,2,1,0:T(8,128)(2,1)} %hist_ref.1, ...), custom_call_target="tpu_custom_call" | custom-call | flops 17179869184 | bytes 12582912 | tf_op jit(solution)/shard_map/pallas_call | solution.py:263
  108.6 3.1 %copy.9 = bf16[32,128,256]{2,1,0:T(8,128)(2,1)} copy(bf16[32,128,256]{2,1,0:T(8,128)(2,1)} %shard_map.73) | data formatting | bytes 4194304
where the time goes:
time: 113 us; the launch traced here: 112 us
  Pallas kernels  109 us (96%)
  local copies, waits for them, and re-layouts  3.13 us (3%)
    pallas_call x1, Pallas kernels, on_device(): pl.pallas_call(functools.partial(kernel, feed_n, chan_n), out_shape=jax.S...  109 us
    unnamed x1, local copies, waits for them, and re-layouts  3.13 us

commit v1 on v0

v1 whole, which is shorter than its diff:
```python
import functools
import math

import jax
import jax.numpy as jnp
import ml_dtypes
import numpy as np
from jax import lax
from jax.experimental import pallas as pl
from jax.experimental.pallas import tpu as pltpu
from jax.sharding import PartitionSpec as P

U = 16
TAPS = 4
TINT = 2
GROUP = 4
WINDOW = 2 * GROUP
PAST = (TAPS - 1) * U
CHUNKS = (2, 4, 4, 2, 2, 1, 1)
STARTS = tuple(sum(CHUNKS[:q]) for q in range(len(CHUNKS)))


def filterbank_table():
    length = TAPS * U
    positions = np.arange(length, dtype=np.float64)
    offsets = (positions - (length - 1) / 2.0) / U
    taper = 0.5 - 0.5 * np.cos(2.0 * math.pi * (positions + 0.5) / length)
    window = np.sinc(offsets) * taper
    window = (window / np.sqrt(np.sum(window * window) / U)).reshape(TAPS, U)
    index_n = np.arange(U)
    phases = 2.0 * math.pi * (index_n[:, None] * index_n[None, :] % U) / U
    cosine, sine = np.cos(phases) / math.sqrt(U), np.sin(phases) / math.sqrt(U)
    parts = [[cosine, -sine], [sine, cosine]]
    table = np.zeros((2, GROUP, U, 2, WINDOW, U))
    for part_in in range(2):
        for part_out in range(2):
            for spectrum in range(GROUP):
                for tap in range(TAPS):
                    table[part_out, spectrum, :, part_in, spectrum + tap, :] = (
                        window[tap][:, None] * parts[part_in][part_out]
                    ).T
    return table.reshape(2 * GROUP * U, 2 * WINDOW * U).astype(ml_dtypes.bfloat16)


def kernel(
    feed_n,
    chan_n,
    table_ref,
    gains_ref,
    lists_ref,
    counts_ref,
    volt_ref,
    hist_ref,
    weight_ref,
    out_ref,
    xbuf,
    stage,
    recv,
    wbuf,
    pick,
    det,
    pstage,
    first_sem,
    main_sem,
    past_sem,
    w_sem,
    feed_send,
    feed_recv,
    chan_send,
    chan_recv,
    self_sem,
):
    me_f, me_c = lax.axis_index("feed"), lax.axis_index("chan")
    chips = feed_n // 2
    my_y, my_core = me_f // 2, me_f % 2
    hops = [(dy, dc) for dy in range(1, chips) for dc in range(2)] + [(0, 1), (0, 0)]
    far = len(hops) - 2
    dests = [lax.rem(my_y + dy, chips) * 2 + lax.rem(my_core + dc, 2) for dy, dc in hops]
    nodes = [lax.rem(me_c + step, chan_n) for step in range(1, chan_n)]

    block = volt_ref.shape[3] // feed_n
    feeds = volt_ref.shape[4]
    beams = weight_ref.shape[3]
    slots = lists_ref.shape[1]
    half = GROUP * U
    group_bins = GROUP // TINT
    early = (CHUNKS[0] + 1) * half

    barrier = pltpu.get_barrier_semaphore()
    for dest in dests[:-1]:
        pl.semaphore_signal(
            barrier, inc=1, device_id={"feed": dest}, device_id_type=pl.DeviceIdType.MESH
        )
    for node in nodes:
        pl.semaphore_signal(
            barrier, inc=1, device_id={"chan": node}, device_id_type=pl.DeviceIdType.MESH
        )

    def main_copy(o, first, size, sem):
        start = pl.multiple_of(dests[o] * block + first, U)
        return pltpu.make_async_copy(
            volt_ref.at[:, :, 0, pl.ds(start, size), :],
            xbuf.at[o, :, :, pl.ds(PAST + first, size), :],
            sem.at[o],
        )

    def first_copy(o):
        return main_copy(o, 0, early, first_sem)

    def rest_copy(o):
        return main_copy(o, early, block - early, main_sem)

    def past_copy(o):
        return pltpu.make_async_copy(
            hist_ref.at[:, :, 0, :, :], xbuf.at[o, :, :, pl.ds(0, PAST), :], past_sem.at[o]
        )

    def load_past(o):
        @pl.when(dests[o] == 0)
        def _():
            past_copy(o).start()

        @pl.when(dests[o] > 0)
        def _():
            first = pl.multiple_of(jnp.maximum(dests[o], 1) * block - PAST, U)
            pltpu.make_async_copy(
                volt_ref.at[:, :, 0, pl.ds(first, PAST), :],
                xbuf.at[o, :, :, pl.ds(0, PAST), :],
                past_sem.at[o],
            ).start()

    for o in range(far):
        load_past(o)
        first_copy(o).start()
    for o in range(far):
        rest_copy(o).start()

    def one_group(o, group):
        first = pl.multiple_of(group * half, half)
        for pol in range(2):
            window = jnp.concatenate(
                [xbuf[o, part, pol, pl.ds(first, WINDOW * U), :] for part in range(2)], axis=0
            )
            spectrum = jnp.dot(table_ref[...], window, preferred_element_type=jnp.float32)
            re, im = spectrum[:half], spectrum[half:]
            gain_re, gain_im = gains_ref[0, pol, :, :], gains_ref[1, pol, :, :]
            cal = (gain_re * re - gain_im * im, gain_re * im + gain_im * re)
            at = pl.ds(pol * half, half)
            for part in range(2):
                if o == feed_n - 1:
                    lanes = pl.ds(pl.multiple_of(me_f * feeds, 128), feeds)
                    recv[group, part, at, lanes] = cal[part].astype(jnp.bfloat16)
                else:
                    stage[o, group, part, at, :] = cal[part].astype(jnp.bfloat16)

    def filterbank(o, q):
        pair = math.gcd(CHUNKS[q], 2)

        def some(step, carry):
            for i in range(pair):
                one_group(o, STARTS[q] + step * pair + i)
            return carry

        lax.fori_loop(0, CHUNKS[q] // pair, some, 0)

    def feed_copy(o, q):
        return pltpu.make_async_remote_copy(
            src_ref=stage.at[o, pl.ds(STARTS[q], CHUNKS[q])],
            dst_ref=recv.at[
                pl.ds(STARTS[q], CHUNKS[q]), :, :, pl.ds(pl.multiple_of(me_f * feeds, 128), feeds)
            ],
            send_sem=feed_send.at[o, q],
            recv_sem=feed_recv.at[o, q],
            device_id={"feed": dests[o]},
            device_id_type=pl.DeviceIdType.MESH,
        )

    def slot_refs(node, q):
        at = pl.ds(STARTS[q] * group_bins, CHUNKS[q] * group_bins)
        return (
            pstage.at[node, at],
            out_ref.at[at, pl.ds(pl.multiple_of(me_c * U, U), U), :],
        )

    def chan_copy(step, q):
        here, there = slot_refs(nodes[step], q)
        return pltpu.make_async_remote_copy(
            src_ref=here,
            dst_ref=there,
            send_sem=chan_send.at[step, q],
            recv_sem=chan_recv.at[step, q],
            device_id={"chan": nodes[step]},
            device_id_type=pl.DeviceIdType.MESH,
        )

    def self_copy(q):
        here, there = slot_refs(me_c, q)
        return pltpu.make_async_copy(here, there, self_sem.at[q])

    for q in range(len(CHUNKS)):
        for o in range(far):
            if q == 0:
                past_copy(o).wait()
                first_copy(o).wait()
            elif q == 1:
                rest_copy(o).wait()
                xbuf[o, :, :, pl.ds(PAST + block, U), :] = jnp.zeros((2, 2, U, feeds), jnp.bfloat16)
            filterbank(o, q)
            if q == 0 and o == 0:
                pl.semaphore_wait(barrier, feed_n - 1 + chan_n - 1)
            feed_copy(o, q).start()
        if q == 0:
            for o in range(far, feed_n):
                load_past(o)
                first_copy(o).start()
                rest_copy(o).start()
            w_copy = pltpu.make_async_copy(weight_ref.at[:, 0], wbuf, w_sem)
            w_copy.start()

    for o in range(far, feed_n):
        past_copy(o).wait()
        first_copy(o).wait()
        rest_copy(o).wait()
        xbuf[o, :, :, pl.ds(PAST + block, U), :] = jnp.zeros((2, 2, U, feeds), jnp.bfloat16)
    for q in range(len(CHUNKS)):
        filterbank(far, q)
        feed_copy(far, q).start()
        filterbank(far + 1, q)

    for node in range(chan_n):
        slot = lax.broadcasted_iota(jnp.int32, (1, slots), 1)
        owned = jnp.where(slot < counts_ref[node], lists_ref[pl.ds(node, 1), :], -1)
        beam = lax.broadcasted_iota(jnp.int32, (beams, slots), 0)
        pick[node] = jnp.where(beam == owned, 1.0, 0.0).astype(jnp.bfloat16)

    w_copy.wait()
    tile = 256

    order = sorted(range(chan_n - 1), key=lambda step: -min(step + 1, chan_n - 1 - step))
    for q in range(len(CHUNKS)):
        for o in range(feed_n - 1):
            feed_copy(o, q).wait_recv()
        groups = slice(STARTS[q], STARTS[q] + CHUNKS[q])
        bins = CHUNKS[q] * group_bins

        def columns(n, inner):
            at = pl.ds(pl.multiple_of(n * tile, tile), tile)
            w_re, w_im = wbuf[0, :, at], wbuf[1, :, at]
            c_re, c_im = (
                recv[groups, part].reshape(CHUNKS[q] * 2 * half, feed_n * feeds) for part in range(2)
            )
            dot = functools.partial(jnp.dot, preferred_element_type=jnp.float32)
            re = dot(c_re, w_re) - dot(c_im, w_im)
            im = dot(c_re, w_im) + dot(c_im, w_re)
            power = (re * re + im * im).reshape(CHUNKS[q], 2, group_bins, TINT, U, tile)
            power = jnp.sum(power[:, 0] + power[:, 1], axis=2) * (1.0 / (4.0 * TINT))
            det[: bins * U, at] = power.reshape(bins * U, tile).astype(jnp.bfloat16)
            return inner

        lax.fori_loop(0, beams // tile, columns, 0)

        def select(node):
            picked = jnp.dot(det[: bins * U], pick[node], preferred_element_type=jnp.float32)
            pstage[node, pl.ds(STARTS[q] * group_bins, bins)] = picked.astype(jnp.bfloat16).reshape(
                bins, U, slots
            )

        for step in order:
            select(nodes[step])
            chan_copy(step, q).start()
        select(me_c)
        self_copy(q).start()

    for q in range(len(CHUNKS)):
        for o in range(feed_n - 1):
            feed_copy(o, q).wait_send()
        for step in range(chan_n - 1):
            chan_copy(step, q).wait()
        self_copy(q).wait()


def on_device(feed_n, chan_n, voltages, history, gains, weights, beam_lists, beam_counts):
    samples, feeds = voltages.shape[3], voltages.shape[4]
    total_feeds, beams = weights.shape[2], weights.shape[3]
    slots = beam_lists.shape[1]
    block = samples // feed_n
    groups = block // U // GROUP
    assert groups == sum(CHUNKS)
    half = GROUP * U
    parts = len(CHUNKS)
    bins = block // U // TINT
    bf16 = jnp.bfloat16
    vmem = pl.BlockSpec(memory_space=pltpu.VMEM)
    hbm = pl.BlockSpec(memory_space=pl.ANY)
    spectra = samples // U
    flops = 2 * 4 * 2 * (block // U) * U * total_feeds * beams
    return pl.pallas_call(
        functools.partial(kernel, feed_n, chan_n),
        out_shape=jax.ShapeDtypeStruct((bins, chan_n * U, slots), bf16),
        in_specs=[vmem, vmem, vmem, pl.BlockSpec(memory_space=pltpu.SMEM), hbm, hbm, hbm],
        out_specs=hbm,
        scratch_shapes=[
            pltpu.VMEM((feed_n, 2, 2, PAST + block + U, feeds), bf16),
            pltpu.VMEM((feed_n - 1, groups, 2, 2 * half, feeds), bf16),
            pltpu.VMEM((groups, 2, 2 * half, total_feeds), bf16),
            pltpu.VMEM((2, total_feeds, beams), bf16),
            pltpu.VMEM((chan_n, beams, slots), bf16),
            pltpu.VMEM((max(CHUNKS) * GROUP // TINT * U, beams), bf16),
            pltpu.VMEM((chan_n, bins, U, slots), bf16),
            pltpu.SemaphoreType.DMA((feed_n,)),
            pltpu.SemaphoreType.DMA((feed_n,)),
            pltpu.SemaphoreType.DMA((feed_n,)),
            pltpu.SemaphoreType.DMA,
            pltpu.SemaphoreType.DMA((feed_n - 1, parts)),
            pltpu.SemaphoreType.DMA((feed_n - 1, parts)),
            pltpu.SemaphoreType.DMA((chan_n - 1, parts)),
            pltpu.SemaphoreType.DMA((chan_n - 1, parts)),
            pltpu.SemaphoreType.DMA((parts,)),
        ],
        compiler_params=pltpu.CompilerParams(
            collective_id=0, has_side_effects=True, vmem_limit_bytes=56 * 2**20
        ),
        cost_estimate=pl.CostEstimate(
            flops=flops, bytes_accessed=4 * spectra * U * feeds * 2 + 4 * total_feeds * beams, transcendentals=0
        ),
    )(
        jnp.asarray(filterbank_table()),
        gains.reshape(2, 2, 1, feeds),
        beam_lists,
        beam_counts,
        voltages,
        history,
        weights,
    )


def solution(mesh):
    in_specs = (
        P(None, None, "chan", None, "feed"),
        P(None, None, "chan", None, "feed"),
        P(None, None, "chan", "feed"),
        P(None, "chan", None, None),
        P(),
        P(),
    )
    out_specs = P("feed", None, "chan")
    body = functools.partial(on_device, mesh.shape["feed"], mesh.shape["chan"])
    return jax.shard_map(body, mesh=mesh, in_specs=in_specs, out_specs=out_specs, check_vma=False)
```

time: 113 us -> 110 us (0.973)
  Pallas kernels: 109 us -> 107 us
    pallas_call x1, Pallas kernels: 109 us -> 107 us  [on_device(): pl.pallas_call(functools.partial(kernel, feed_n, chan_n), out_shape=jax.S...]
where the time goes in v1:
time: 110 us
  Pallas kernels  107 us (97%)
  local copies, waits for them, and re-layouts  3.13 us (3%)
    pallas_call x1, Pallas kernels, on_device(): pl.pallas_call(functools.partial(kernel, feed_n, chan_n), out_shape=jax.S...  107 us
    unnamed x1, local copies, waits for them, and re-layouts  3.13 us

profile of v1, /device:TPU:0, one launch (start us, length us, event | category | flops | bytes accessed | tf_op | source)
XLA Modules:
  0.0 109.8 jit_solution(9531881258726504238)
XLA Ops:
  0.0 106.6 %shard_map.73 = bf16[32,128,256]{2,1,0:T(8,128)(2,1)} custom-call(bf16[128,256]{1,0:T(8,128)(2,1)} %constant.2.clone.table_ref, f32[2,2,1,256]{3,2,1,0:T(1,128)} %gains_ref.1, s32[8,256]{1,0:T(8,128)} %lists_ref.1, s32[8]{0:T(128)} %counts_ref.1, bf16[2,2,1,4096,256]{4,3,2,1,0:T(8,128)(2,1)} %volt_ref.1, bf16[2,2,1,48,256]{4,3,2,1,0:T(8,128)(2,1)} %hist_ref.1, ...), custom_call_target="tpu_custom_call" | custom-call | flops 17179869184 | bytes 12582912 | tf_op jit(solution)/shard_map/pallas_call | solution.py:297
  106.6 3.1 %copy.9 = bf16[32,128,256]{2,1,0:T(8,128)(2,1)} copy(bf16[32,128,256]{2,1,0:T(8,128)(2,1)} %shard_map.73) | data formatting | bytes 4194304
